TPU v7x, 32 devices: a whole 2x2x4 slice. The times are simulated.
32 devices in a mesh: scen: 2 (over y), gx: 4 (over z), gy: 4 (over x, core).
Axes of the slice: x: 2, y: 2, z: 4, core: 2. Of those that a mesh axis runs over, the one named last changes fastest.
Arguments:
- head_old: float32 [80, 64, 512], P('scen', 'gx', 'gy'), parts along dimension 0, may hold values from -3 to 1
- soil_class: int32 [40, 64, 512], P(None, 'gx', 'gy'), may hold values from 0 to 11
- ksat_table: float32 [12], replicated, may hold values from 0.05 to 2
- alpha_table: float32 [12], replicated, may hold values from 0.3 to 2
- capacity_table: float32 [12], replicated, may hold values from 0.2 to 2
- rain: float32 [128, 512], P(('scen', 'gx'), 'gy'), parts along dimension 0, may hold values from 0.1 to 2
- lake_level: float32 [128], P('scen'), parts along dimension 0, may hold values from 0 to 2
- pit_id: int32 [64, 512], P('gx', 'gy'), may hold values from 0 to 127, as said below
Outputs:
- head_new: float32 [80, 64, 512], P('scen', 'gx', 'gy'), parts along dimension 0
- boundary: float32 [128, 512], P(('scen', 'gx'), 'gy'), parts along dimension 0
- lake_new: float32 [128], P('scen'), parts along dimension 0
There are 2 independent parts, one for each index of `scen`. A program takes and returns all parts, laid end to end along the dimension named above; an argument that names none is the same for every part. Nothing has to cross between parts.
Inputs may be any that keep to these rules, and one draw needn't show every extreme that they name: `pit_id`: values under 64 name a pit; larger values mark columns without a pit; a pit may own no column.
All inputs are finite; a program needn't handle non-finite values.
Results may differ from a plain program's by a relative error of at most 0.0001.
Values sent between devices are 32-bit elements; how exact they have to be, the bound alone decides.
A program may use at most 64 MiB of HBM per device.

v0:
```python
import jax
import jax.numpy as jnp
from jax import lax
from jax.sharding import PartitionSpec as P

ITERS = 2
NPIT = 64


LEAK = 0.5
VERT = 2.0


def with_halo(block, sides, width):
    for axis, dim in sides:
        count = lax.axis_size(axis)
        forward = [(i, i + 1) for i in range(count - 1)]
        backward = [(target, source) for source, target in forward]
        low = lax.ppermute(
            lax.slice_in_dim(block, block.shape[dim] - width, None, axis=dim), axis, forward
        )
        high = lax.ppermute(lax.slice_in_dim(block, 0, width, axis=dim), axis, backward)
        block = jnp.concatenate([low, block, high], axis=dim)
    return block


def harmonic(first, second):
    return 2.0 * first * second / (first + second)


def lookup_tables(classes, ksat_table, alpha_table, capacity_table):
    ksat_cell = jnp.zeros(classes.shape, jnp.float32)
    alpha_cell = jnp.zeros(classes.shape, jnp.float32)
    capacity_cell = jnp.zeros(classes.shape, jnp.float32)
    for which in range(ksat_table.shape[0]):
        match = classes == which
        ksat_cell = jnp.where(match, ksat_table[which], ksat_cell)
        alpha_cell = jnp.where(match, alpha_table[which], alpha_cell)
        capacity_cell = jnp.where(match, capacity_table[which], capacity_cell)
    return (ksat_cell, alpha_cell, capacity_cell)


def make_operator(store, extra, tx, ty, tz):

    def apply_padded(padded, field):
        fx = tx * (padded[:, 1:, 1:-1] - padded[:, :-1, 1:-1])
        fy = ty * (padded[:, 1:-1, 1:] - padded[:, 1:-1, :-1])
        fz = tz * (field[1:] - field[:-1])
        out = (store + extra) * field
        out = out + fx[:, :-1, :] - fx[:, 1:, :]
        out = out + fy[:, :, :-1] - fy[:, :, 1:]
        out = out + jnp.pad(fz, ((1, 0), (0, 0), (0, 0))) - jnp.pad(fz, ((0, 1), (0, 0), (0, 0)))
        return out

    def operate(field):
        padded = with_halo(field, (("gx", 1), ("gy", 2)), 1)
        return apply_padded(padded, field)

    return (apply_padded, operate)


def precond_norm(residual, precond):
    return lax.psum(jnp.sum(residual * precond), ("gx", "gy"))


def shards(head_old, soil_class, ksat_table, alpha_table, capacity_table, rain, lake_level, pit_id):
    ksat_cell, alpha_cell, capacity_cell = lookup_tables(
        soil_class, ksat_table, alpha_table, capacity_table
    )
    relative = jnp.exp(alpha_cell * jnp.minimum(head_old, 0.0))
    cond = ksat_cell * relative
    store = capacity_cell * relative
    inpit = pit_id < NPIT
    onehot = (pit_id[None, :, :] == jnp.arange(NPIT, dtype=jnp.int32)[:, None, None]).astype(
        jnp.float32
    )
    lake_cell = jnp.sum(onehot * lake_level[:, None, None], axis=0)
    leak_top = jnp.where(inpit, jnp.float32(LEAK), jnp.float32(0.0))
    extra = jnp.zeros_like(head_old).at[0].set(leak_top)
    wide = with_halo(cond, (("gx", 1), ("gy", 2)), 1)
    tx = harmonic(wide[:, :-1, 1:-1], wide[:, 1:, 1:-1])
    ty = harmonic(wide[:, 1:-1, :-1], wide[:, 1:-1, 1:])
    tz = VERT * harmonic(cond[:-1], cond[1:])
    diag = store + extra + tx[:, :-1, :] + tx[:, 1:, :] + ty[:, :, :-1] + ty[:, :, 1:]
    diag = diag + jnp.pad(tz, ((1, 0), (0, 0), (0, 0))) + jnp.pad(tz, ((0, 1), (0, 0), (0, 0)))
    apply_padded, operate = make_operator(store, extra, tx, ty, tz)
    rhs = (store * head_old).at[0].add(rain + LEAK * lake_cell)
    solution = head_old
    start_image = operate(head_old)
    residual = rhs - start_image
    precond = residual / diag
    direction = precond
    norm_now = precond_norm(residual, precond)
    for step in range(ITERS):
        image = operate(direction)
        alpha = norm_now / lax.psum(jnp.sum(direction * image), ("gx", "gy"))
        solution = solution + alpha * direction
        residual = residual - alpha * image
        if step + 1 < ITERS:
            precond = residual / diag
            norm_next = precond_norm(residual, precond)
            direction = precond + norm_next / norm_now * direction
            norm_now = norm_next
    top = solution[0]
    seep = jnp.where(inpit, LEAK * (lake_cell - top), jnp.float32(0.0))
    outflow, inflow, area = lax.psum(
        (
            jnp.sum(onehot * seep[None], axis=(1, 2)),
            jnp.sum(onehot * rain[None], axis=(1, 2)),
            jnp.sum(onehot, axis=(1, 2)),
        ),
        ("gx", "gy"),
    )
    lake_new = lake_level + (inflow - outflow) / jnp.maximum(area, 1.0)
    boundary = jnp.where(inpit, jnp.sum(onehot * lake_new[:, None, None], axis=0), top)
    return (solution, boundary, lake_new)


def solution(mesh):
    return jax.shard_map(
        shards,
        mesh=mesh,
        in_specs=(
            P("scen", "gx", "gy"),
            P(None, "gx", "gy"),
            P(),
            P(),
            P(),
            P(("scen", "gx"), "gy"),
            P("scen"),
            P("gx", "gy"),
        ),
        out_specs=(P("scen", "gx", "gy"), P(("scen", "gx"), "gy"), P("scen")),
        check_vma=False,
    )
```

profile of v0, /device:TPU:0, one launch (start us, length us, event | category | flops | bytes accessed | tf_op | source)
XLA Modules:
  0.0 238.1 jit_solution(12985021580080587027)
XLA Ops:
  0.6 1.8 fusion.40
  3.2 17.2 %select_multiply_fusion = (f32[40,16,128]{2,1,0:T(8,128)S(1)}, pred[40,16,128]{2,1,0:T(8,128)(4,1)S(1)}, pred[40,16,128]{2,1,0:T(8,128)(4,1)S(1)}, pred[40,16,12...) fusion(f32[]{:T(128)} %bitcast.37, f32[]{:T(128)} %bitcast.36, ...), kind=kLoop, calls=%fused_computation.83 | loop fusion | flops 3194880 | bytes 1966176 | tf_op jit(solution)/shard_map/mul | solution.py:71
  20.4 4.9 %collective-permute-start = (f32[40,1,128]{2,1,0:T(1,128)S(1)}, f32[40,1,128]{2,1,0:T(1,128)S(1)}, u32[]{:S(2)}, u32[]{:S(2)}) collective-permute-start(f32[40,1,128]{2,1,0:T(1,128)S(1)} %get-tuple-element.76), channel_id=1, source_target_pairs={{0,4},{4,8},{8,12},{1,5},{5,9},{9,13},{2,6},{6,10},{10,14},{3,7},{... | collective-permute-start | bytes 61448 | tf_op jit(solution)/shard_map/ppermute | solution.py:19
  25.3 1.3 collective-permute-start.1
  26.6 1.3 collective-permute-start.2
  27.9 5.2 %collective-permute-start.3 = (f32[40,1,128]{2,1,0:T(1,128)S(1)}, f32[40,1,128]{2,1,0:T(1,128)S(1)}, u32[]{:S(2)}, u32[]{:S(2)}) collective-permute-start(f32[40,1,128]{2,1,0:T(1,128)S(1)} %get-tuple-element.78), channel_id=1, source_target_pairs={{0,4},{4,8},{8,12},{1,5},{5,9},{9,13},{2,6},{6,10},{10,14},{3,7},{... | collective-permute-start | bytes 61448 | tf_op jit(solution)/shard_map/ppermute | solution.py:19
  34.7 15.8 %fusion.30 = (f32[40,16,128]{2,1,0:T(8,128)S(1)}, f32[40,16,128]{2,1,0:T(8,128)S(1)}) fusion(f32[40,16,128]{2,1,0:T(8,128)S(1)} %copy-done, pred[40,16,128]{2,1,0:T(8,128)(4,1)S(1)} %get-tuple-element.59, pred[40,16,128]{2,1,0:T(8,128)(4,1)S(1)} %get-tuple-element.58, pred[40,16,128]{2,1,0:T(8,128)(4,1)S(1)} %get-tuple-element.57, ...), kind=kLoop, calls=%fused_computation.115 | loop fusion | flops 2293760 | bytes 1966176 | tf_op jit(solution)/shard_map/mul | solution.py:87
  50.7 1.3 collective-permute-start.4
  52.1 1.3 collective-permute-start.5
  53.7 1.3 collective-permute-start.6
  55.0 5.4 %collective-permute-start.7 = (f32[40,18,1]{2,1,0:T(8,128)S(1)}, f32[40,18,1]{2,1,0:T(8,128)S(1)}, u32[]{:S(2)}, u32[]{:S(2)}) collective-permute-start(f32[40,18,1]{2,1,0:T(8,128)S(1)} %get-tuple-element.69), channel_id=1, source_target_pairs={{0,1},{1,2},{2,3},{4,5},{5,6},{6,7},{8,9},{9,10},{10,11},{12,13},{... | collective-permute-start | bytes 8648 | tf_op jit(solution)/shard_map/ppermute | solution.py:19
  62.8 1.3 collective-permute-start.8
  64.1 4.6 %collective-permute-start.9 = (f32[40,1,128]{2,1,0:T(1,128)S(1)}, f32[40,1,128]{2,1,0:T(1,128)S(1)}, u32[]{:S(2)}, u32[]{:S(2)}) collective-permute-start(f32[40,1,128]{2,1,0:T(1,128)S(1)} %get-tuple-element.74), channel_id=1, source_target_pairs={{0,4},{4,8},{8,12},{1,5},{5,9},{9,13},{2,6},{6,10},{10,14},{3,7},{... | collective-permute-start | bytes 61448 | tf_op jit(solution)/shard_map/ppermute | solution.py:19
  68.8 1.4 collective-permute-done.9
  70.4 1.3 collective-permute-start.10
  71.7 9.6 %collective-permute-start.11 = (f32[40,18,1]{2,1,0:T(8,128)S(1)}, f32[40,18,1]{2,1,0:T(8,128)S(1)}, u32[]{:S(2)}, u32[]{:S(2)}) collective-permute-start(f32[40,18,1]{2,1,0:T(8,128)S(1)} %get-tuple-element.65), channel_id=1, source_target_pairs={{0,1},{1,2},{2,3},{4,5},{5,6},{6,7},{8,9},{9,10},{10,11},{12,13},{... | collective-permute-start | bytes 8648 | tf_op jit(solution)/shard_map/ppermute | solution.py:19
  84.0 37.6 %all-reduce.9 = (f32[]{:T(128)}, f32[]{:T(128)}) all-reduce(f32[]{:T(128)} %get-tuple-element.28, f32[]{:T(128)} %get-tuple-element.27), channel_id=1, replica_groups=mesh['scen'=2,'gx'=4,'gy'=4] {'gx','gy'}, use_global_device_ids=true, to_apply=%region_2.3 | all-reduce | flops 2 | bytes 16 | tf_op jit(solution)/shard_map/psum | solution.py:63
  123.6 30.4 %psum.51 = f32[]{:T(128)} all-reduce(f32[]{:T(128)} %multiply_reduce_fusion), channel_id=1, replica_groups=mesh['scen'=2,'gx'=4,'gy'=4] {'gx','gy'}, use_global_device_ids=true, to_apply=%region_6.7 | all-reduce | flops 1 | bytes 8 | tf_op jit(solution)/shard_map/psum | solution.py:63
  156.5 1.3 collective-permute-start.12
  157.8 4.5 %collective-permute-start.13 = (f32[40,1,128]{2,1,0:T(1,128)S(1)}, f32[40,1,128]{2,1,0:T(1,128)S(1)}, u32[]{:S(2)}, u32[]{:S(2)}) collective-permute-start(f32[40,1,128]{2,1,0:T(1,128)S(1)} %get-tuple-element.72), channel_id=1, source_target_pairs={{0,4},{4,8},{8,12},{1,5},{5,9},{9,13},{2,6},{6,10},{10,14},{3,7},{... | collective-permute-start | bytes 61448 | tf_op jit(solution)/shard_map/ppermute | solution.py:19
  162.4 1.4 collective-permute-done.13
  165.4 3.1 %collective-permute-start.15 = (f32[40,18,1]{2,1,0:T(8,128)S(1)}, f32[40,18,1]{2,1,0:T(8,128)S(1)}, u32[]{:S(2)}, u32[]{:S(2)}) collective-permute-start(f32[40,18,1]{2,1,0:T(8,128)S(1)} %get-tuple-element.63), channel_id=1, source_target_pairs={{0,1},{1,2},{2,3},{4,5},{5,6},{6,7},{8,9},{9,10},{10,11},{12,13},{... | collective-permute-start | bytes 8648 | tf_op jit(solution)/shard_map/ppermute | solution.py:19
  171.1 34.4 %psum.52 = f32[]{:T(128)} all-reduce(f32[]{:T(128)} %fusion.12), channel_id=1, replica_groups=mesh['scen'=2,'gx'=4,'gy'=4] {'gx','gy'}, use_global_device_ids=true, to_apply=%region_8.9 | all-reduce | flops 1 | bytes 8 | tf_op jit(solution)/shard_map/psum | solution.py:96
  207.5 29.5 %all-reduce.8 = (f32[64]{0:T(128)S(1)}, f32[64]{0:T(128)S(1)}, f32[64]{0:T(128)S(1)}) all-reduce(f32[64]{0:T(128)S(1)} %get-tuple-element.30, f32[64]{0:T(128)S(1)} %get-tuple-element.31, f32[64]{0:T(128)S(1)} %get-tuple-element.29), channel_id=1, replica_groups=mesh['scen'=2,'gx'=4,'gy'=4] {'gx','gy'}, use_global_device_ids=true, to_apply=%region_14.15 | all-reduce | flops 192 | bytes 1536 | tf_op jit(solution)/shard_map/psum | solution.py:106
  (69 shorter events, 16.0 us)
Async XLA Ops:
  0.6 1.8 copy-start.4
  3.2 23.4 %copy-start = (f32[40,16,128]{2,1,0:T(8,128)S(1)}, f32[40,16,128]{2,1,0:T(8,128)}, u32[]{:S(2)}) copy-start(f32[40,16,128]{2,1,0:T(8,128)} %param.12) | copy-start | bytes 983044
  20.4 30.1 %collective-permute-start = (f32[40,1,128]{2,1,0:T(1,128)S(1)}, f32[40,1,128]{2,1,0:T(1,128)S(1)}, u32[]{:S(2)}, u32[]{:S(2)}) collective-permute-start(f32[40,1,128]{2,1,0:T(1,128)S(1)} %get-tuple-element.76), channel_id=1, source_target_pairs={{0,4},{4,8},{8,12},{1,5},{5,9},{9,13},{2,6},{6,10},{10,14},{3,7},{... | collective-permute-start | bytes 61448 | tf_op jit(solution)/shard_map/ppermute | solution.py:19
  25.3 25.2 %collective-permute-start.1 = (f32[40,1,128]{2,1,0:T(1,128)S(1)}, f32[40,1,128]{2,1,0:T(1,128)S(1)}, u32[]{:S(2)}, u32[]{:S(2)}) collective-permute-start(f32[40,1,128]{2,1,0:T(1,128)S(1)} %get-tuple-element.77), channel_id=1, source_target_pairs={{4,0},{8,4},{12,8},{5,1},{9,5},{13,9},{6,2},{10,6},{14,10},{7,3},{... | collective-permute-start | bytes 61448 | tf_op jit(solution)/shard_map/ppermute | solution.py:22
  26.6 26.7 %collective-permute-start.2 = (f32[40,1,128]{2,1,0:T(1,128)S(1)}, f32[40,1,128]{2,1,0:T(1,128)S(1)}, u32[]{:S(2)}, u32[]{:S(2)}) collective-permute-start(f32[40,1,128]{2,1,0:T(1,128)S(1)} %get-tuple-element.79), channel_id=1, source_target_pairs={{4,0},{8,4},{12,8},{5,1},{9,5},{13,9},{6,2},{10,6},{14,10},{7,3},{... | collective-permute-start | bytes 61448 | tf_op jit(solution)/shard_map/ppermute | solution.py:22
  27.9 25.4 %collective-permute-start.3 = (f32[40,1,128]{2,1,0:T(1,128)S(1)}, f32[40,1,128]{2,1,0:T(1,128)S(1)}, u32[]{:S(2)}, u32[]{:S(2)}) collective-permute-start(f32[40,1,128]{2,1,0:T(1,128)S(1)} %get-tuple-element.78), channel_id=1, source_target_pairs={{0,4},{4,8},{8,12},{1,5},{5,9},{9,13},{2,6},{6,10},{10,14},{3,7},{... | collective-permute-start | bytes 61448 | tf_op jit(solution)/shard_map/ppermute | solution.py:19
  33.1 0.7 copy-start.5
  33.8 0.7 copy-start.3
  33.8 0.7 copy-start.7
  34.6 15.8 %copy-start.6 = (f32[16,128]{1,0:T(8,128)S(1)}, f32[16,128]{1,0:T(8,128)}, u32[]{:S(2)}) copy-start(f32[16,128]{1,0:T(8,128)} %param.17) | copy-start | bytes 24580
  50.7 9.8 %collective-permute-start.4 = (f32[40,18,1]{2,1,0:T(8,128)S(1)}, f32[40,18,1]{2,1,0:T(8,128)S(1)}, u32[]{:S(2)}, u32[]{:S(2)}) collective-permute-start(f32[40,18,1]{2,1,0:T(8,128)S(1)} %get-tuple-element.66), channel_id=1, source_target_pairs={{0,1},{1,2},{2,3},{4,5},{5,6},{6,7},{8,9},{9,10},{10,11},{12,13},{... | collective-permute-start | bytes 8648 | tf_op jit(solution)/shard_map/ppermute | solution.py:19
  52.1 8.5 %collective-permute-start.5 = (f32[40,18,1]{2,1,0:T(8,128)S(1)}, f32[40,18,1]{2,1,0:T(8,128)S(1)}, u32[]{:S(2)}, u32[]{:S(2)}) collective-permute-start(f32[40,18,1]{2,1,0:T(8,128)S(1)} %get-tuple-element.67), channel_id=1, source_target_pairs={{1,0},{2,1},{3,2},{5,4},{6,5},{7,6},{9,8},{10,9},{11,10},{13,12},{... | collective-permute-start | bytes 8648 | tf_op jit(solution)/shard_map/ppermute | solution.py:22
  53.7 6.9 %collective-permute-start.6 = (f32[40,18,1]{2,1,0:T(8,128)S(1)}, f32[40,18,1]{2,1,0:T(8,128)S(1)}, u32[]{:S(2)}, u32[]{:S(2)}) collective-permute-start(f32[40,18,1]{2,1,0:T(8,128)S(1)} %get-tuple-element.68), channel_id=1, source_target_pairs={{1,0},{2,1},{3,2},{5,4},{6,5},{7,6},{9,8},{10,9},{11,10},{13,12},{... | collective-permute-start | bytes 8648 | tf_op jit(solution)/shard_map/ppermute | solution.py:22
  55.0 6.8 %collective-permute-start.7 = (f32[40,18,1]{2,1,0:T(8,128)S(1)}, f32[40,18,1]{2,1,0:T(8,128)S(1)}, u32[]{:S(2)}, u32[]{:S(2)}) collective-permute-start(f32[40,18,1]{2,1,0:T(8,128)S(1)} %get-tuple-element.69), channel_id=1, source_target_pairs={{0,1},{1,2},{2,3},{4,5},{5,6},{6,7},{8,9},{9,10},{10,11},{12,13},{... | collective-permute-start | bytes 8648 | tf_op jit(solution)/shard_map/ppermute | solution.py:19
  62.8 5.9 %collective-permute-start.8 = (f32[40,1,128]{2,1,0:T(1,128)S(1)}, f32[40,1,128]{2,1,0:T(1,128)S(1)}, u32[]{:S(2)}, u32[]{:S(2)}) collective-permute-start(f32[40,1,128]{2,1,0:T(1,128)S(1)} %get-tuple-element.75), channel_id=1, source_target_pairs={{4,0},{8,4},{12,8},{5,1},{9,5},{13,9},{6,2},{10,6},{14,10},{7,3},{... | collective-permute-start | bytes 61448 | tf_op jit(solution)/shard_map/ppermute | solution.py:22
  64.1 6.0 %collective-permute-start.9 = (f32[40,1,128]{2,1,0:T(1,128)S(1)}, f32[40,1,128]{2,1,0:T(1,128)S(1)}, u32[]{:S(2)}, u32[]{:S(2)}) collective-permute-start(f32[40,1,128]{2,1,0:T(1,128)S(1)} %get-tuple-element.74), channel_id=1, source_target_pairs={{0,4},{4,8},{8,12},{1,5},{5,9},{9,13},{2,6},{6,10},{10,14},{3,7},{... | collective-permute-start | bytes 61448 | tf_op jit(solution)/shard_map/ppermute | solution.py:19
  70.4 11.1 %collective-permute-start.10 = (f32[40,18,1]{2,1,0:T(8,128)S(1)}, f32[40,18,1]{2,1,0:T(8,128)S(1)}, u32[]{:S(2)}, u32[]{:S(2)}) collective-permute-start(f32[40,18,1]{2,1,0:T(8,128)S(1)} %get-tuple-element.64), channel_id=1, source_target_pairs={{1,0},{2,1},{3,2},{5,4},{6,5},{7,6},{9,8},{10,9},{11,10},{13,12},{... | collective-permute-start | bytes 8648 | tf_op jit(solution)/shard_map/ppermute | solution.py:22
  71.7 11.0 %collective-permute-start.11 = (f32[40,18,1]{2,1,0:T(8,128)S(1)}, f32[40,18,1]{2,1,0:T(8,128)S(1)}, u32[]{:S(2)}, u32[]{:S(2)}) collective-permute-start(f32[40,18,1]{2,1,0:T(8,128)S(1)} %get-tuple-element.65), channel_id=1, source_target_pairs={{0,1},{1,2},{2,3},{4,5},{5,6},{6,7},{8,9},{9,10},{10,11},{12,13},{... | collective-permute-start | bytes 8648 | tf_op jit(solution)/shard_map/ppermute | solution.py:19
  84.0 39.7 %copy-start.1 = (f32[40,16,128]{2,1,0:T(8,128)}, f32[40,16,128]{2,1,0:T(8,128)S(1)}, u32[]{:S(2)}) copy-start(f32[40,16,128]{2,1,0:T(8,128)S(1)} %get-tuple-element.37) | copy-start | bytes 983044
  156.5 5.9 %collective-permute-start.12 = (f32[40,1,128]{2,1,0:T(1,128)S(1)}, f32[40,1,128]{2,1,0:T(1,128)S(1)}, u32[]{:S(2)}, u32[]{:S(2)}) collective-permute-start(f32[40,1,128]{2,1,0:T(1,128)S(1)} %get-tuple-element.73), channel_id=1, source_target_pairs={{4,0},{8,4},{12,8},{5,1},{9,5},{13,9},{6,2},{10,6},{14,10},{7,3},{... | collective-permute-start | bytes 61448 | tf_op jit(solution)/shard_map/ppermute | solution.py:22
  157.8 6.0 %collective-permute-start.13 = (f32[40,1,128]{2,1,0:T(1,128)S(1)}, f32[40,1,128]{2,1,0:T(1,128)S(1)}, u32[]{:S(2)}, u32[]{:S(2)}) collective-permute-start(f32[40,1,128]{2,1,0:T(1,128)S(1)} %get-tuple-element.72), channel_id=1, source_target_pairs={{0,4},{4,8},{8,12},{1,5},{5,9},{9,13},{2,6},{6,10},{10,14},{3,7},{... | collective-permute-start | bytes 61448 | tf_op jit(solution)/shard_map/ppermute | solution.py:19
  164.1 4.6 %collective-permute-start.14 = (f32[40,18,1]{2,1,0:T(8,128)S(1)}, f32[40,18,1]{2,1,0:T(8,128)S(1)}, u32[]{:S(2)}, u32[]{:S(2)}) collective-permute-start(f32[40,18,1]{2,1,0:T(8,128)S(1)} %get-tuple-element.62), channel_id=1, source_target_pairs={{1,0},{2,1},{3,2},{5,4},{6,5},{7,6},{9,8},{10,9},{11,10},{13,12},{... | collective-permute-start | bytes 8648 | tf_op jit(solution)/shard_map/ppermute | solution.py:22
  165.4 4.5 %collective-permute-start.15 = (f32[40,18,1]{2,1,0:T(8,128)S(1)}, f32[40,18,1]{2,1,0:T(8,128)S(1)}, u32[]{:S(2)}, u32[]{:S(2)}) collective-permute-start(f32[40,18,1]{2,1,0:T(8,128)S(1)} %get-tuple-element.63), channel_id=1, source_target_pairs={{0,1},{1,2},{2,3},{4,5},{5,6},{6,7},{8,9},{9,10},{10,11},{12,13},{... | collective-permute-start | bytes 8648 | tf_op jit(solution)/shard_map/ppermute | solution.py:19
  206.9 31.2 %copy-start.2 = (f32[40,16,128]{2,1,0:T(8,128)}, f32[40,16,128]{2,1,0:T(8,128)S(1)}, u32[]{:S(2)}) copy-start(f32[40,16,128]{2,1,0:T(8,128)S(1)} %multiply_add_fusion) | copy-start | bytes 983044
  (1 other events, 0.5 us)
where the time goes:
time: 239 us; the launch traced here: 238 us
  blocking collectives  132 us (55%)
  starting transfers between devices  48.9 us (20%)
  other arithmetic  40.7 us (17%)
  waiting for transfers between devices  6.38 us (3%)
  local copies, waits for them, and re-layouts  5.07 us (2%)
  between operations  5.05 us (2%)
    psum x2, blocking collectives, precond_norm(): return lax.psum(jnp.sum(residual * precond), ('gx', 'gy'))  68.1 us
    ppermute x8, starting transfers between devices, with_halo(): lax.ppermute(lax.slice_in_dim(block, block.shape[dim] - width, None, axis...  38.6 us
    psum x1, blocking collectives, shards(): alpha = norm_now / lax.psum(jnp.sum(direction * image), ('gx', 'gy'))  34.4 us
    psum x1, blocking collectives, shards(): lax.psum((jnp.sum(onehot * seep[None], axis=(1, 2)), jnp.sum(onehot * rai...  29.5 us
    mul x1, other arithmetic, shards(): cond = ksat_cell * relative  17.2 us
    mul x1, other arithmetic, shards(): rhs = (store * head_old).at[0].add(rain + LEAK * lake_cell)  15.8 us
    ppermute x8, starting transfers between devices, with_halo(): lax.ppermute(lax.slice_in_dim(block, 0, width, axis=dim), axis, backward)  10.3 us
    ppermute x8, waiting for transfers between devices, with_halo(): lax.ppermute(lax.slice_in_dim(block, block.shape[dim] - width, None, axis...  6.36 us
  transfers between devices with their start and end apart: 16, of which 5 were waited for; matrix products, arithmetic and copies ran while one was open for 8% of the time, Pallas kernels for 0%

commit v1 on v0

v1 whole, which is shorter than its diff:
```python
import functools

import jax
import jax.numpy as jnp
from jax import lax
from jax.experimental import pallas as pl
from jax.experimental.pallas import tpu as pltpu
from jax.sharding import PartitionSpec as P

NPIT = 64
LEAK = 0.5
VERT = 2.0
CH = 4
MESH = pl.DeviceIdType.MESH
HIGH = lax.Precision.HIGHEST


def harmonic(first, second):
    return 2.0 * first * second / (first + second)


def kernel(
    nx, ny, lz, rows,
    head_hbm, soil_hbm, ksat_ref, alpha_ref, cap_ref, rain_ref, lake_ref, pit_ref,
    out_hbm, bnd_ref, lake_out_ref,
    H, SC, C, DG, TX, TY, TZ, R, Z, NZ, U, M,
    xs1, xr1, ys1, yr1, xs2, xr2, ys2, yr2, xs3, xr3, ys3, yr3,
    gather,
    local_sem, send_sem, recv_sem, ar_send, ar_recv,
):
    f32 = jnp.float32
    mx, my = lax.axis_index("gx"), lax.axis_index("gy")
    n = nx * ny
    me = mx * ny + my
    cells = lz * rows
    lo_pad = rows
    step_rows = CH * rows
    steps = lz // CH

    in_h = pltpu.make_async_copy(head_hbm, H.at[pl.ds(lo_pad, cells)], local_sem.at[0])
    in_s = pltpu.make_async_copy(soil_hbm, SC, local_sem.at[1])
    in_h.start()
    in_s.start()

    def peer(s):
        other = lax.rem(me + s, n)
        return {"gx": lax.div(other, ny), "gy": lax.rem(other, ny)}

    def each_peer(body):
        if n <= 16:
            for s in range(1, n):
                body(s)
        else:
            lax.fori_loop(1, n, lambda s, c: (body(s), c)[1], 0)

    barrier = pltpu.get_barrier_semaphore()
    each_peer(lambda s: pl.semaphore_signal(barrier, inc=1, device_id=peer(s), device_id_type=MESH))

    has = {("x", 0): mx > 0, ("x", 1): mx < nx - 1, ("y", 0): my > 0, ("y", 1): my < ny - 1}
    dev = {
        ("x", 0): {"gx": jnp.maximum(mx - 1, 0)},
        ("x", 1): {"gx": jnp.minimum(mx + 1, nx - 1)},
        ("y", 0): {"gy": jnp.maximum(my - 1, 0)},
        ("y", 1): {"gy": jnp.minimum(my + 1, ny - 1)},
    }

    def copy(ax, side, src, dst, number):
        return pltpu.make_async_remote_copy(
            src_ref=src.at[side], dst_ref=dst.at[1 - side],
            send_sem=send_sem.at[number + side], recv_sem=recv_sem.at[number + 1 - side],
            device_id=dev[ax, side], device_id_type=MESH,
        )

    def send(ax, src, dst, number, sides=(0, 1)):
        for side in sides:
            @pl.when(has[ax, side])
            def _(side=side):
                copy(ax, side, src, dst, number).start()

    def receive(ax, src, dst, number, sides=(0, 1)):
        for side in sides:
            @pl.when(has[ax, side])
            def _(side=side):
                copy(ax, 1 - side, src, dst, number).wait_recv()

    def sent(ax, src, dst, number, sides=(0, 1)):
        for side in sides:
            @pl.when(has[ax, side])
            def _(side=side):
                copy(ax, side, src, dst, number).wait_send()

    for ax, buf in (("x", xr1), ("y", yr1), ("x", xr2), ("y", yr2)):
        for side in (0, 1):
            @pl.when(jnp.logical_not(has[ax, side]))
            def _(buf=buf, side=side):
                buf[side] = jnp.zeros(buf.shape[1:], f32)
    for ax, buf in (("x", xr3), ("y", yr3)):
        @pl.when(jnp.logical_not(has[ax, 1]))
        def _(buf=buf):
            buf[1] = jnp.zeros(buf.shape[1:], f32)

    for ref in (H, C, Z, U):
        ref[pl.ds(0, rows), :] = jnp.zeros((rows, 128), f32)
        ref[pl.ds(lo_pad + cells, rows), :] = jnp.zeros((rows, 128), f32)
    TZ[pl.ds(0, rows), :] = jnp.zeros((rows, 128), f32)

    pit = pit_ref[...]
    for i in range(rows):
        ids = lax.broadcasted_iota(jnp.int32, (128, 128), 0)
        M[:, i * 128:(i + 1) * 128] = jnp.where(ids == pit[i:i + 1, :], f32(1), f32(0))

    def spread(row):
        flat = jnp.dot(jnp.broadcast_to(row, (8, 128)), M[...], precision=HIGH, preferred_element_type=f32)
        return jnp.concatenate([flat[0:1, i * 128:(i + 1) * 128] for i in range(rows)], axis=0)

    def flatten(field):
        return jnp.concatenate([field[i:i + 1, :] for i in range(rows)], axis=1)

    def by_pit(flat):
        return lax.dot_general(flat, M[...], (((1,), (1,)), ((), ())), precision=HIGH, preferred_element_type=f32)

    def at(k, shift=0):
        return pl.ds(pl.multiple_of(lo_pad + k * step_rows + shift * rows, rows), step_rows)

    def at0(k):
        return pl.ds(pl.multiple_of(k * step_rows, rows), step_rows)

    in_h.wait()
    in_s.wait()

    @pl.loop(0, steps)
    def _(k):
        classes = SC[at0(k), :]
        ks = jnp.zeros(classes.shape, f32)
        al = jnp.zeros(classes.shape, f32)
        cp = jnp.zeros(classes.shape, f32)
        for which in range(ksat_ref.shape[0]):
            match = classes == which
            ks = jnp.where(match, ksat_ref[which], ks)
            al = jnp.where(match, alpha_ref[which], al)
            cp = jnp.where(match, cap_ref[which], cp)
        relative = jnp.exp(al * jnp.minimum(H[at(k), :], 0.0))
        C[at(k), :] = ks * relative
        DG[at0(k), :] = cp * relative

    def edge(ref, which, pad):
        return ref[pl.ds(pad + which, lz, stride=rows), :]

    c_first, c_last = edge(C, 0, lo_pad), edge(C, rows - 1, lo_pad)
    h_first, h_last = edge(H, 0, lo_pad), edge(H, rows - 1, lo_pad)
    xs1[0, 0], xs1[0, 1] = c_first, h_first
    xs1[1, 0], xs1[1, 1] = c_last, h_last

    def columns(ref, pad):
        turned = ref[pl.ds(pad, cells), :].T
        return turned[0:1, :], turned[127:128, :]

    def to_block(low, high):
        r = lax.broadcasted_iota(jnp.int32, (8, cells), 0)
        top = jnp.where(r == 0, low, f32(0))
        bottom = jnp.where(r == 7, high, f32(0))
        return jnp.concatenate([top, jnp.zeros((112, cells), f32), bottom], axis=0).T

    pl.semaphore_wait(barrier, n - 1)
    send("x", xs1, xr1, 0)
    cy = columns(C, lo_pad)
    hy = columns(H, lo_pad)
    for side in (0, 1):
        ys1[side, 0:1, :] = cy[side]
        ys1[side, 1:2, :] = hy[side]
    send("y", ys1, yr1, 2)

    shape3 = (CH, rows, 128)
    lane = lax.broadcasted_iota(jnp.int32, shape3, 2)
    sub = lax.broadcasted_iota(jnp.int32, shape3, 1)

    def rx(v, s):
        return pltpu.roll(v, s % rows, 1)

    def ry(v, s):
        return pltpu.roll(v, s % 128, 2)

    def get(ref, k, shift=0):
        return ref[at(k, shift), :].reshape(shape3)

    def get0(ref, k):
        return ref[at0(k), :].reshape(shape3)

    def put0(ref, k, v):
        ref[at0(k), :] = v.reshape(step_rows, 128)

    def put(ref, k, v):
        ref[at(k), :] = v.reshape(step_rows, 128)

    @pl.loop(0, steps)
    def _(k):
        c, h = get(C, k), get(H, k)
        tx = jnp.where(sub == rows - 1, 0.0, harmonic(c, rx(c, -1)))
        ty = jnp.where(lane == 127, 0.0, harmonic(c, ry(c, -1)))
        tz = VERT * harmonic(c, get(C, k, 1))
        put0(TX, k, tx)
        put0(TY, k, ty)
        put(TZ, k, tz)
        fx = tx * (rx(h, -1) - h)
        fy = ty * (ry(h, -1) - h)
        fz = tz * (get(H, k, 1) - h)
        tz_low = get(TZ, k, -1)
        fz_low = tz_low * (h - get(H, k, -1))
        put0(DG, k, get0(DG, k) + tx + rx(tx, 1) + ty + ry(ty, 1) + tz + tz_low)
        put0(R, k, fx - rx(fx, 1) + fy - ry(fy, 1) + fz - fz_low)

    inpit = pit < NPIT
    lake_row = lake_ref[...]
    lake_wide = jnp.concatenate([lake_row, jnp.zeros((1, 128 - NPIT), f32)], axis=1)
    lake_cell = spread(lake_wide)
    top_h = H[pl.ds(lo_pad, rows), :]
    rain = rain_ref[...]
    top_rows = pl.ds(0, rows)
    DG[top_rows, :] += jnp.where(inpit, f32(LEAK), f32(0))
    R[top_rows, :] += rain + jnp.where(inpit, LEAK * (lake_cell - top_h), f32(0))
    r8 = lax.broadcasted_iota(jnp.int32, (8, rows * 128), 0)
    early = by_pit(jnp.where(r8 == 0, flatten(rain), jnp.where(r8 == 1, f32(1), flatten(top_h))))

    receive("x", xs1, xr1, 0)
    tx_low = harmonic(c_first, xr1[0, 0])
    tx_high = harmonic(c_last, xr1[1, 0])
    first = pl.ds(0, lz, stride=rows)
    last = pl.ds(rows - 1, lz, stride=rows)
    DG[first, :] += tx_low
    DG[last, :] += tx_high
    R[first, :] += tx_low * (xr1[0, 1] - h_first)
    R[last, :] += tx_high * (xr1[1, 1] - h_last)
    receive("y", ys1, yr1, 2)
    ty_low = harmonic(cy[0], yr1[0, 0:1, :])
    ty_high = harmonic(cy[1], yr1[1, 0:1, :])
    NZ[...] = to_block(ty_low, ty_high)
    U[pl.ds(lo_pad, cells), :] = to_block(
        ty_low * (yr1[0, 1:2, :] - hy[0]), ty_high * (yr1[1, 1:2, :] - hy[1])
    )

    zero_acc = jnp.zeros(shape3, f32)

    def make_z(k, acc):
        inverse = 1.0 / (get0(DG, k) + get0(NZ, k))
        r = get0(R, k) + get(U, k)
        z = r * inverse
        put0(DG, k, inverse)
        put0(R, k, r)
        put(Z, k, z)
        return acc + r * z

    acc_a = lax.fori_loop(0, steps, make_z, zero_acc)

    xs2[0] = edge(Z, 0, lo_pad)
    xs2[1] = edge(Z, rows - 1, lo_pad)
    send("x", xs2, xr2, 4)
    zy = columns(Z, lo_pad)
    for side in (0, 1):
        ys2[side] = zy[side]
    send("y", ys2, yr2, 6)

    @pl.loop(0, steps)
    def _(k):
        z, tx, ty = get(Z, k), get0(TX, k), get0(TY, k)
        out = tx * rx(z, -1) + rx(tx * z, 1)
        out = out + ty * ry(z, -1) + ry(ty * z, 1)
        put0(NZ, k, out + get(TZ, k) * get(Z, k, 1) + get(TZ, k, -1) * get(Z, k, -1))

    ones8 = jnp.zeros((8, rows * 128), f32)
    mid = by_pit(flatten(Z[pl.ds(lo_pad, rows), :]) + ones8)

    receive("x", xs2, xr2, 4)
    NZ[first, :] += tx_low * xr2[0]
    NZ[last, :] += tx_high * xr2[1]
    receive("y", ys2, yr2, 6)
    U[pl.ds(lo_pad, cells), :] = to_block(ty_low * yr2[0], ty_high * yr2[1])

    def make_u(k, acc):
        nz = get0(NZ, k) + get(U, k)
        u = nz * get0(DG, k)
        put(U, k, u)
        return acc[0] + get0(R, k) * u, acc[1] + nz * u

    acc_g, acc_c = lax.fori_loop(0, steps, make_u, (zero_acc, zero_acc))

    xs3[0] = edge(U, 0, lo_pad)
    send("x", xs3, xr3, 8, (0,))
    uy = columns(U, lo_pad)
    ys3[0] = uy[0]
    send("y", ys3, yr3, 10, (0,))

    def make_f(k, acc):
        u = get(U, k)
        inner = get0(TX, k) * rx(u, -1) + get0(TY, k) * ry(u, -1) + get(TZ, k) * get(U, k, 1)
        return acc + u * inner

    acc_f = lax.fori_loop(0, steps, make_f, zero_acc)
    late = by_pit(flatten(U[pl.ds(lo_pad, rows), :]) + ones8)

    def row_sum(acc):
        return jnp.sum(jnp.sum(acc, axis=0), axis=0, keepdims=True)

    sum_a, sum_g, sum_c, sum_f = row_sum(acc_a), row_sum(acc_g), row_sum(acc_c), row_sum(acc_f)
    u_last = edge(U, rows - 1, lo_pad)
    receive("x", xs3, xr3, 8, (1,))
    sum_f = sum_f + jnp.sum(u_last * tx_high * xr3[1], axis=0, keepdims=True)
    receive("y", ys3, yr3, 10, (1,))
    cross = uy[1] * ty_high * yr3[1]
    for i in range(cells // 128):
        sum_f = sum_f + cross[:, i * 128:(i + 1) * 128]
    sum_f = 2.0 * sum_f

    r1 = lax.broadcasted_iota(jnp.int32, (8, 128), 0)
    l1 = lax.broadcasted_iota(jnp.int32, (8, 128), 1)
    scal = jnp.where(r1 == 0, sum_a, jnp.where(r1 == 1, sum_g, jnp.where(r1 == 2, sum_c, sum_f)))
    scal = scal + pltpu.roll(scal, 64, 1)
    pits = jnp.where(r1 < 3, early, jnp.where(r1 == 3, mid, late))
    gather[me] = jnp.where(l1 < NPIT, pits, scal)

    def reduce_copy(s):
        return pltpu.make_async_remote_copy(
            src_ref=gather.at[me], dst_ref=gather.at[me], send_sem=ar_send.at[s], recv_sem=ar_recv.at[me],
            device_id=peer(s), device_id_type=MESH,
        )

    def arrival(s):
        source = lax.rem(me + s, n)
        return pltpu.make_async_remote_copy(
            src_ref=gather.at[source], dst_ref=gather.at[source], send_sem=ar_send.at[s], recv_sem=ar_recv.at[source],
            device_id=peer(s), device_id_type=MESH,
        )

    each_peer(lambda s: reduce_copy(s).start())
    each_peer(lambda s: arrival(s).wait_recv())
    if n <= 16:
        total = gather[0]
        for j in range(1, n):
            total = total + gather[j]
    else:
        total = lax.fori_loop(1, n, lambda j, t: t + gather[j], gather[0])

    scalars = jnp.sum(jnp.where(l1 < NPIT, f32(0), total), axis=1, keepdims=True)
    a, g, c, f = (scalars[i:i + 1, :] for i in range(4))
    b = a - g
    step0 = a / b
    ratio = (a * c - g * g) / (b * b)
    p = ratio - g / b
    step1 = a * ratio / (p * p * b + 2.0 * p * step0 * (g - c) + step0 * step0 * (c - f))
    coef_z = step0 + step1 * p
    coef_u = step1 * step0

    coef_z3, coef_u3 = coef_z.reshape(1, 1, 1), coef_u.reshape(1, 1, 1)

    @pl.loop(0, steps)
    def _(k):
        put0(NZ, k, get(H, k) + coef_z3 * get(Z, k) + coef_u3 * get(U, k))

    out_copy = pltpu.make_async_copy(NZ, out_hbm, local_sem.at[0])
    out_copy.start()

    inflow, area = total[0:1, :NPIT], total[1:2, :NPIT]
    top_sum = total[2:3, :NPIT] + coef_z * total[3:4, :NPIT] + coef_u * total[4:5, :NPIT]
    outflow = LEAK * (lake_row * area - top_sum)
    lake_new = lake_row + (inflow - outflow) / jnp.maximum(area, 1.0)
    lake_out_ref[...] = lake_new
    lake_new_cell = spread(jnp.concatenate([lake_new, jnp.zeros((1, 128 - NPIT), f32)], axis=1))
    bnd_ref[...] = jnp.where(inpit, lake_new_cell, NZ[pl.ds(0, rows), :])

    sent("x", xs1, xr1, 0)
    sent("y", ys1, yr1, 2)
    sent("x", xs2, xr2, 4)
    sent("y", ys2, yr2, 6)
    sent("x", xs3, xr3, 8, (0,))
    sent("y", ys3, yr3, 10, (0,))
    each_peer(lambda s: reduce_copy(s).wait_send())
    out_copy.wait()


def solution(mesh):
    nx, ny = mesh.shape["gx"], mesh.shape["gy"]

    def shards(head_old, soil_class, ksat_table, alpha_table, capacity_table, rain, lake_level, pit_id):
        lz, rows, width = head_old.shape
        cells = lz * rows
        f32 = jnp.float32
        block = pltpu.VMEM((cells, width), f32)
        padded = pltpu.VMEM((cells + 2 * rows, width), f32)
        vmem = pl.BlockSpec(memory_space=pltpu.VMEM)
        smem = pl.BlockSpec(memory_space=pltpu.SMEM)
        hbm = pl.BlockSpec(memory_space=pl.ANY)
        n = nx * ny
        out, boundary, lake_new = pl.pallas_call(
            functools.partial(kernel, nx, ny, lz, rows),
            out_shape=(
                jax.ShapeDtypeStruct((cells, width), f32),
                jax.ShapeDtypeStruct((rows, width), f32),
                jax.ShapeDtypeStruct((1, NPIT), f32),
            ),
            in_specs=[hbm, hbm, smem, smem, smem, vmem, vmem, vmem],
            out_specs=(hbm, vmem, vmem),
            scratch_shapes=[
                padded, pltpu.VMEM((cells, width), jnp.int32), padded, block, block, block, padded,
                block, padded, block, padded, pltpu.VMEM((128, rows * 128), f32),
                pltpu.VMEM((2, 2, lz, width), f32), pltpu.VMEM((2, 2, lz, width), f32),
                pltpu.VMEM((2, 2, cells), f32), pltpu.VMEM((2, 2, cells), f32),
                pltpu.VMEM((2, lz, width), f32), pltpu.VMEM((2, lz, width), f32),
                pltpu.VMEM((2, 1, cells), f32), pltpu.VMEM((2, 1, cells), f32),
                pltpu.VMEM((2, lz, width), f32), pltpu.VMEM((2, lz, width), f32),
                pltpu.VMEM((2, 1, cells), f32), pltpu.VMEM((2, 1, cells), f32),
                pltpu.VMEM((n, 8, 128), f32),
                pltpu.SemaphoreType.DMA((2,)),
                pltpu.SemaphoreType.DMA((12,)), pltpu.SemaphoreType.DMA((12,)),
                pltpu.SemaphoreType.DMA((n,)), pltpu.SemaphoreType.DMA((n,)),
            ],
            compiler_params=pltpu.CompilerParams(
                collective_id=0, has_side_effects=True, vmem_limit_bytes=40 * 1024 * 1024
            ),
            name="step",
        )(
            head_old.reshape(cells, width), soil_class.reshape(cells, width),
            ksat_table, alpha_table, capacity_table, rain, lake_level.reshape(1, NPIT), pit_id,
        )
        return out.reshape(lz, rows, width), boundary, lake_new.reshape(NPIT)

    return jax.shard_map(
        shards,
        mesh=mesh,
        in_specs=(
            P("scen", "gx", "gy"),
            P(None, "gx", "gy"),
            P(),
            P(),
            P(),
            P(("scen", "gx"), "gy"),
            P("scen"),
            P("gx", "gy"),
        ),
        out_specs=(P("scen", "gx", "gy"), P(("scen", "gx"), "gy"), P("scen")),
        check_vma=False,
    )
```

time: 239 us -> 28.7 us (0.12)
  blocking collectives: 132 us -> 0 us
  starting transfers between devices: 48.9 us -> 0 us
  other arithmetic: 40.7 us -> 0 us
  Pallas kernels: 0 us -> 21.9 us
  waiting for transfers between devices: 6.38 us -> 0 us
  between operations: 5.05 us -> 0.68 us
    psum x4 -> x0, blocking collectives: 132 us -> none  [the longest x2 68.1 us: precond_norm(): return lax.psum(jnp.sum(residual * precond), ('gx', 'gy'))]
    ppermute x16 -> x0, starting transfers between devices: 48.9 us -> none  [the longest x8 38.6 us: with_halo(): lax.ppermute(lax.slice_in_dim(block, block.shape[dim] - width, None, axis...]
    mul x11 -> x0, other arithmetic: 35.1 us -> none  [the longest x1 17.2 us: shards(): cond = ksat_cell * relative]
    pallas_call x0 -> x1, Pallas kernels: none -> 21.9 us  [shards(): pl.pallas_call(functools.partial(kernel, nx, ny, lz, rows), out_shape=(ja...]
    ppermute x16 -> x0, waiting for transfers between devices: 6.38 us -> none  [the longest x8 6.36 us: with_halo(): lax.ppermute(lax.slice_in_dim(block, block.shape[dim] - width, None, axis...]
    unnamed x18 -> x19, local copies, waits for them, and re-layouts: 0.95 us -> 5.84 us
    slice x11 -> x0, local copies, waits for them, and re-layouts: 4.11 us -> none  [the longest x1 1.8 us: lookup_tables(): alpha_cell = jnp.where(match, alpha_table[which], alpha_cell)]
    reduce_sum x6 -> x0, other arithmetic: 3.17 us -> none  [the longest x2 1.64 us: shards(): alpha = norm_now / lax.psum(jnp.sum(direction * image), ('gx', 'gy'))]
  transfers between devices with their start and end apart: 16 -> 0, of which waited for: 5 -> 0; matrix products, arithmetic and copies ran while one was open for 8% -> 0% of each run, Pallas kernels for 0% -> 0%
where the time goes in v1:
time: 28.7 us; the launch traced here: 28.4 us
  Pallas kernels  21.9 us (76%)
  local copies, waits for them, and re-layouts  5.84 us (20%)
  between operations  0.68 us (2%)
    pallas_call x1, Pallas kernels, shards(): pl.pallas_call(functools.partial(kernel, nx, ny, lz, rows), out_shape=(ja...  21.9 us
    unnamed x19, local copies, waits for them, and re-layouts  5.84 us

profile of v1, /device:TPU:0, one launch (start us, length us, event | category | flops | bytes accessed | tf_op | source)
XLA Modules:
  0.0 28.4 jit_solution(15026949159945616381)
XLA Ops:
  0.6 0.0 copy-start.7
  0.6 0.0 copy-start.4
  0.7 0.0 copy-start.5
  0.7 0.0 copy-start.6
  0.7 0.6 %copy-done.7 = f32[64]{0:T(128)S(1)} copy-done((f32[64]{0:T(128)S(1)}, f32[64]{0:T(128)}, u32[]{:S(2)}) %copy-start.7) | copy-done | bytes 280
  1.3 0.0 copy-done.4
  1.3 0.0 copy-done.5
  1.3 0.0 copy-done.6
  1.3 0.0 copy-start
  1.3 1.0 %copy-done = f32[40,16,128]{2,1,0:T(8,128)S(1)} copy-done((f32[40,16,128]{2,1,0:T(8,128)S(1)}, f32[40,16,128]{2,1,0:T(8,128)}, u32[]{:S(2)}) %copy-start) | copy-done | bytes 327704
  2.3 0.0 copy-start.1
  2.3 1.0 %copy-done.1 = s32[40,16,128]{2,1,0:T(8,128)S(1)} copy-done((s32[40,16,128]{2,1,0:T(8,128)S(1)}, s32[40,16,128]{2,1,0:T(8,128)}, u32[]{:S(2)}) %copy-start.1) | copy-done | bytes 327704
  3.3 0.0 copy-start.2
  3.3 0.7 %copy-done.2 = f32[16,128]{1,0:T(8,128)S(1)} copy-done((f32[16,128]{1,0:T(8,128)S(1)}, f32[16,128]{1,0:T(8,128)}, u32[]{:S(2)}) %copy-start.2) | copy-done | bytes 8216
  4.0 0.0 copy-start.3
  4.0 0.7 %copy-done.3 = s32[16,128]{1,0:T(8,128)S(1)} copy-done((s32[16,128]{1,0:T(8,128)S(1)}, s32[16,128]{1,0:T(8,128)}, u32[]{:S(2)}) %copy-start.3) | copy-done | bytes 8216
  4.7 21.9 %step.1 = (f32[640,128]{1,0:T(8,128)S(1)}, f32[16,128]{1,0:T(8,128)S(1)}, f32[1,64]{1,0:T(1,128)S(1)}) custom-call(f32[640,128]{1,0:T(8,128)S(1)} %bitcast.5, s32[640,128]{1,0:T(8,128)S(1)} %bitcast.6, f32[12]{0:T(128)S(1)} %copy-done.4, f32[12]{0:T(128)S(1)} %copy-done.5, f32[12]{0:T(128)S(1)} %copy-done.6, f32[16,128]{1,0:T(8,128)S(1)} %copy-done.2, ...), custom_call_target="tpu_custom_call" | custom-call | tf_op jit(solution)/shard_map/step/pallas_call | solution.py:392
  26.6 0.7 %copy.14 = f32[40,16,128]{2,1,0:T(8,128)} copy(f32[40,16,128]{2,1,0:T(8,128)S(1)} %bitcast.7) | data formatting | bytes 655360
  27.3 0.6 %copy.15 = f32[16,128]{1,0:T(8,128)} copy(f32[16,128]{1,0:T(8,128)S(1)} %get-tuple-element.13) | data formatting | bytes 16384
  27.9 0.5 %copy.16 = f32[64]{0:T(128)} copy(f32[64]{0:T(128)S(1)} %bitcast.9) | data formatting | bytes 512
Async XLA Ops:
  0.6 0.7 %copy-start.7 = (f32[64]{0:T(128)S(1)}, f32[64]{0:T(128)}, u32[]{:S(2)}) copy-start(f32[64]{0:T(128)} %param.14) | copy-start | bytes 772
  0.6 0.7 %copy-start.4 = (f32[12]{0:T(128)S(1)}, f32[12]{0:T(128)}, u32[]{:S(2)}) copy-start(f32[12]{0:T(128)} %ksat_ref.1) | copy-start | bytes 148
  0.7 0.7 %copy-start.5 = (f32[12]{0:T(128)S(1)}, f32[12]{0:T(128)}, u32[]{:S(2)}) copy-start(f32[12]{0:T(128)} %alpha_ref.1) | copy-start | bytes 148
  0.7 0.7 %copy-start.6 = (f32[12]{0:T(128)S(1)}, f32[12]{0:T(128)}, u32[]{:S(2)}) copy-start(f32[12]{0:T(128)} %cap_ref.1) | copy-start | bytes 148
  1.3 1.0 %copy-start = (f32[40,16,128]{2,1,0:T(8,128)S(1)}, f32[40,16,128]{2,1,0:T(8,128)}, u32[]{:S(2)}) copy-start(f32[40,16,128]{2,1,0:T(8,128)} %param.8) | copy-start | bytes 983044
  2.3 1.0 %copy-start.1 = (s32[40,16,128]{2,1,0:T(8,128)S(1)}, s32[40,16,128]{2,1,0:T(8,128)}, u32[]{:S(2)}) copy-start(s32[40,16,128]{2,1,0:T(8,128)} %param.9) | copy-start | bytes 983044
  3.3 0.7 %copy-start.2 = (f32[16,128]{1,0:T(8,128)S(1)}, f32[16,128]{1,0:T(8,128)}, u32[]{:S(2)}) copy-start(f32[16,128]{1,0:T(8,128)} %rain_ref.1) | copy-start | bytes 24580
  4.0 0.7 %copy-start.3 = (s32[16,128]{1,0:T(8,128)S(1)}, s32[16,128]{1,0:T(8,128)}, u32[]{:S(2)}) copy-start(s32[16,128]{1,0:T(8,128)} %pit_ref.1) | copy-start | bytes 24580

commit v2 on v1

--- a/solution.py
+++ b/solution.py
@@ -10,7 +10,7 @@
 NPIT = 64
 LEAK = 0.5
 VERT = 2.0
-CH = 4
+CH = 20
 MESH = pl.DeviceIdType.MESH
 HIGH = lax.Precision.HIGHEST
 
@@ -21,9 +21,9 @@
 
 def kernel(
     nx, ny, lz, rows,
-    head_hbm, soil_hbm, ksat_ref, alpha_ref, cap_ref, rain_ref, lake_ref, pit_ref,
-    out_hbm, bnd_ref, lake_out_ref,
-    H, SC, C, DG, TX, TY, TZ, R, Z, NZ, U, M,
+    head_hbm, soil_hbm, ksat_hbm, alpha_hbm, cap_hbm, rain_hbm, lake_hbm, pit_hbm,
+    out_ref, bnd_ref, lake_out_ref,
+    ksat_ref, alpha_ref, cap_ref, rain_ref, lake_ref, pit_ref, H, SC, C, DG, TX, TY, TZ, R, Z, NZ, U, M,
     xs1, xr1, ys1, yr1, xs2, xr2, ys2, yr2, xs3, xr3, ys3, yr3,
     gather,
     local_sem, send_sem, recv_sem, ar_send, ar_recv,
@@ -39,8 +39,15 @@
 
     in_h = pltpu.make_async_copy(head_hbm, H.at[pl.ds(lo_pad, cells)], local_sem.at[0])
     in_s = pltpu.make_async_copy(soil_hbm, SC, local_sem.at[1])
-    in_h.start()
-    in_s.start()
+    small = [
+        pltpu.make_async_copy(src, dst, local_sem.at[2 + i])
+        for i, (src, dst) in enumerate((
+            (ksat_hbm, ksat_ref), (alpha_hbm, alpha_ref), (cap_hbm, cap_ref),
+            (rain_hbm, rain_ref), (lake_hbm, lake_ref), (pit_hbm, pit_ref),
+        ))
+    ]
+    for each in small[:3] + [in_s, in_h] + small[3:]:
+        each.start()
 
     def peer(s):
         other = lax.rem(me + s, n)
@@ -104,11 +111,6 @@
         ref[pl.ds(lo_pad + cells, rows), :] = jnp.zeros((rows, 128), f32)
     TZ[pl.ds(0, rows), :] = jnp.zeros((rows, 128), f32)
 
-    pit = pit_ref[...]
-    for i in range(rows):
-        ids = lax.broadcasted_iota(jnp.int32, (128, 128), 0)
-        M[:, i * 128:(i + 1) * 128] = jnp.where(ids == pit[i:i + 1, :], f32(1), f32(0))
-
     def spread(row):
         flat = jnp.dot(jnp.broadcast_to(row, (8, 128)), M[...], precision=HIGH, preferred_element_type=f32)
         return jnp.concatenate([flat[0:1, i * 128:(i + 1) * 128] for i in range(rows)], axis=0)
@@ -125,8 +127,10 @@
     def at0(k):
         return pl.ds(pl.multiple_of(k * step_rows, rows), step_rows)
 
+    for each in small[:3]:
+        each.wait()
+    in_s.wait()
     in_h.wait()
-    in_s.wait()
 
     @pl.loop(0, steps)
     def _(k):
@@ -209,6 +213,13 @@
         put0(DG, k, get0(DG, k) + tx + rx(tx, 1) + ty + ry(ty, 1) + tz + tz_low)
         put0(R, k, fx - rx(fx, 1) + fy - ry(fy, 1) + fz - fz_low)
 
+    for each in small[3:]:
+        each.wait()
+    pit = pit_ref[...]
+    for i in range(rows):
+        ids = lax.broadcasted_iota(jnp.int32, (128, 128), 0)
+        M[:, i * 128:(i + 1) * 128] = jnp.where(ids == pit[i:i + 1, :], f32(1), f32(0))
+
     inpit = pit < NPIT
     lake_row = lake_ref[...]
     lake_wide = jnp.concatenate([lake_row, jnp.zeros((1, 128 - NPIT), f32)], axis=1)
@@ -353,10 +364,7 @@
 
     @pl.loop(0, steps)
     def _(k):
-        put0(NZ, k, get(H, k) + coef_z3 * get(Z, k) + coef_u3 * get(U, k))
-
-    out_copy = pltpu.make_async_copy(NZ, out_hbm, local_sem.at[0])
-    out_copy.start()
+        put0(out_ref, k, get(H, k) + coef_z3 * get(Z, k) + coef_u3 * get(U, k))
 
     inflow, area = total[0:1, :NPIT], total[1:2, :NPIT]
     top_sum = total[2:3, :NPIT] + coef_z * total[3:4, :NPIT] + coef_u * total[4:5, :NPIT]
@@ -364,7 +372,7 @@
     lake_new = lake_row + (inflow - outflow) / jnp.maximum(area, 1.0)
     lake_out_ref[...] = lake_new
     lake_new_cell = spread(jnp.concatenate([lake_new, jnp.zeros((1, 128 - NPIT), f32)], axis=1))
-    bnd_ref[...] = jnp.where(inpit, lake_new_cell, NZ[pl.ds(0, rows), :])
+    bnd_ref[...] = jnp.where(inpit, lake_new_cell, out_ref[pl.ds(0, rows), :])
 
     sent("x", xs1, xr1, 0)
     sent("y", ys1, yr1, 2)
@@ -373,7 +381,15 @@
     sent("x", xs3, xr3, 8, (0,))
     sent("y", ys3, yr3, 10, (0,))
     each_peer(lambda s: reduce_copy(s).wait_send())
-    out_copy.wait()
+
+
+def write_out(a_ref, b_ref, c_ref, a_out, b_out, c_out, sems):
+    pairs = ((a_ref, a_out), (b_ref, b_out), (c_ref, c_out))
+    copies = [pltpu.make_async_copy(src, dst, sems.at[i]) for i, (src, dst) in enumerate(pairs)]
+    for each in copies:
+        each.start()
+    for each in copies:
+        each.wait()
 
 
 def solution(mesh):
@@ -386,19 +402,21 @@
         block = pltpu.VMEM((cells, width), f32)
         padded = pltpu.VMEM((cells + 2 * rows, width), f32)
         vmem = pl.BlockSpec(memory_space=pltpu.VMEM)
-        smem = pl.BlockSpec(memory_space=pltpu.SMEM)
-        hbm = pl.BlockSpec(memory_space=pl.ANY)
+        hbm = pl.BlockSpec(memory_space=pltpu.HBM)
         n = nx * ny
-        out, boundary, lake_new = pl.pallas_call(
+        shapes = (
+            jax.ShapeDtypeStruct((cells, width), f32),
+            jax.ShapeDtypeStruct((rows, width), f32),
+            jax.ShapeDtypeStruct((1, NPIT), f32),
+        )
+        results = pl.pallas_call(
             functools.partial(kernel, nx, ny, lz, rows),
-            out_shape=(
-                jax.ShapeDtypeStruct((cells, width), f32),
-                jax.ShapeDtypeStruct((rows, width), f32),
-                jax.ShapeDtypeStruct((1, NPIT), f32),
-            ),
-            in_specs=[hbm, hbm, smem, smem, smem, vmem, vmem, vmem],
-            out_specs=(hbm, vmem, vmem),
+            out_shape=shapes,
+            in_specs=[hbm] * 8,
+            out_specs=(vmem, vmem, vmem),
             scratch_shapes=[
+                pltpu.SMEM(ksat_table.shape, f32), pltpu.SMEM(ksat_table.shape, f32), pltpu.SMEM(ksat_table.shape, f32),
+                pltpu.VMEM((rows, width), f32), pltpu.VMEM((1, NPIT), f32), pltpu.VMEM((rows, width), jnp.int32),
                 padded, pltpu.VMEM((cells, width), jnp.int32), padded, block, block, block, padded,
                 block, padded, block, padded, pltpu.VMEM((128, rows * 128), f32),
                 pltpu.VMEM((2, 2, lz, width), f32), pltpu.VMEM((2, 2, lz, width), f32),
@@ -408,18 +426,21 @@
                 pltpu.VMEM((2, lz, width), f32), pltpu.VMEM((2, lz, width), f32),
                 pltpu.VMEM((2, 1, cells), f32), pltpu.VMEM((2, 1, cells), f32),
                 pltpu.VMEM((n, 8, 128), f32),
-                pltpu.SemaphoreType.DMA((2,)),
+                pltpu.SemaphoreType.DMA((8,)),
                 pltpu.SemaphoreType.DMA((12,)), pltpu.SemaphoreType.DMA((12,)),
                 pltpu.SemaphoreType.DMA((n,)), pltpu.SemaphoreType.DMA((n,)),
             ],
             compiler_params=pltpu.CompilerParams(
-                collective_id=0, has_side_effects=True, vmem_limit_bytes=40 * 1024 * 1024
+                collective_id=0, has_side_effects=True, vmem_limit_bytes=16 * 1024 * 1024
             ),
             name="step",
         )(
-            head_old.reshape(cells, width), soil_class.reshape(cells, width),
-            ksat_table, alpha_table, capacity_table, rain, lake_level.reshape(1, NPIT), pit_id,
+            *(pltpu.with_memory_space_constraint(x, pltpu.HBM) for x in (
+                head_old.reshape(cells, width), soil_class.reshape(cells, width),
+                ksat_table, alpha_table, capacity_table, rain, lake_level.reshape(1, NPIT), pit_id,
+            ))
         )
+        out, boundary, lake_new = results
         return out.reshape(lz, rows, width), boundary, lake_new.reshape(NPIT)
 
     return jax.shard_map(

time: 28.7 us -> 23 us (0.80)
  local copies, waits for them, and re-layouts: 5.84 us -> 1.84 us
  Pallas kernels: 21.9 us -> 20.4 us
    unnamed x19 -> x3, local copies, waits for them, and re-layouts: 5.84 us -> 1.84 us
    pallas_call x1, Pallas kernels: 21.9 us -> 20.4 us  [shards(): pl.pallas_call(functools.partial(kernel, nx, ny, lz, rows), out_shape=sha...]
where the time goes in v2:
time: 23 us; the launch traced here: 22.9 us
  Pallas kernels  20.4 us (89%)
  local copies, waits for them, and re-layouts  1.84 us (8%)
  between operations  0.64 us (3%)
    pallas_call x1, Pallas kernels, shards(): pl.pallas_call(functools.partial(kernel, nx, ny, lz, rows), out_shape=sha...  20.4 us
    unnamed x3, local copies, waits for them, and re-layouts  1.84 us

profile of v2, /device:TPU:0, one launch (start us, length us, event | category | flops | bytes accessed | tf_op | source)
XLA Modules:
  0.0 22.9 jit_solution(5576078276312039618)
XLA Ops:
  0.6 20.4 %step.1 = (f32[640,128]{1,0:T(8,128)S(1)}, f32[16,128]{1,0:T(8,128)S(1)}, f32[1,64]{1,0:T(1,128)S(1)}) custom-call(f32[640,128]{1,0:T(8,128)} %bitcast.7, s32[640,128]{1,0:T(8,128)} %bitcast.8, f32[12]{0:T(128)} %ksat_hbm.1, f32[12]{0:T(128)} %alpha_hbm.1, f32[12]{0:T(128)} %cap_hbm.1, f32[16,128]{1,0:T(8,128)} %rain_hbm.1, f32[1,64]{1,0:T(1,128)} %bitcast.9, ...), custom_call_target="tpu_custom_call" | custom-call | tf_op jit(solution)/shard_map/step/pallas_call | solution.py:412
  21.0 0.7 %copy.14 = f32[40,16,128]{2,1,0:T(8,128)} copy(f32[40,16,128]{2,1,0:T(8,128)S(1)} %bitcast.5) | data formatting | bytes 655360
  21.8 0.6 %copy.15 = f32[16,128]{1,0:T(8,128)} copy(f32[16,128]{1,0:T(8,128)S(1)} %get-tuple-element.13) | data formatting | bytes 16384
  22.4 0.5 %copy.16 = f32[64]{0:T(128)} copy(f32[64]{0:T(128)S(1)} %bitcast.6) | data formatting | bytes 512

commit v3 on v2

--- a/solution.py
+++ b/solution.py
@@ -12,7 +12,6 @@
 VERT = 2.0
 CH = 20
 MESH = pl.DeviceIdType.MESH
-HIGH = lax.Precision.HIGHEST
 
 
 def harmonic(first, second):
@@ -23,7 +22,7 @@
     nx, ny, lz, rows,
     head_hbm, soil_hbm, ksat_hbm, alpha_hbm, cap_hbm, rain_hbm, lake_hbm, pit_hbm,
     out_ref, bnd_ref, lake_out_ref,
-    ksat_ref, alpha_ref, cap_ref, rain_ref, lake_ref, pit_ref, H, SC, C, DG, TX, TY, TZ, R, Z, NZ, U, M,
+    ksat_ref, alpha_ref, cap_ref, rain_ref, lake_ref, pit_ref, H, SC, C, DG, TX, TY, TZ, R, Z, NZ, U,
     xs1, xr1, ys1, yr1, xs2, xr2, ys2, yr2, xs3, xr3, ys3, yr3,
     gather,
     local_sem, send_sem, recv_sem, ar_send, ar_recv,
@@ -110,16 +109,6 @@
         ref[pl.ds(0, rows), :] = jnp.zeros((rows, 128), f32)
         ref[pl.ds(lo_pad + cells, rows), :] = jnp.zeros((rows, 128), f32)
     TZ[pl.ds(0, rows), :] = jnp.zeros((rows, 128), f32)
-
-    def spread(row):
-        flat = jnp.dot(jnp.broadcast_to(row, (8, 128)), M[...], precision=HIGH, preferred_element_type=f32)
-        return jnp.concatenate([flat[0:1, i * 128:(i + 1) * 128] for i in range(rows)], axis=0)
-
-    def flatten(field):
-        return jnp.concatenate([field[i:i + 1, :] for i in range(rows)], axis=1)
-
-    def by_pit(flat):
-        return lax.dot_general(flat, M[...], (((1,), (1,)), ((), ())), precision=HIGH, preferred_element_type=f32)
 
     def at(k, shift=0):
         return pl.ds(pl.multiple_of(lo_pad + k * step_rows + shift * rows, rows), step_rows)
@@ -216,9 +205,22 @@
     for each in small[3:]:
         each.wait()
     pit = pit_ref[...]
-    for i in range(rows):
-        ids = lax.broadcasted_iota(jnp.int32, (128, 128), 0)
-        M[:, i * 128:(i + 1) * 128] = jnp.where(ids == pit[i:i + 1, :], f32(1), f32(0))
+    ids = lax.broadcasted_iota(jnp.int32, (NPIT, 128), 0)
+
+    def spread(row):
+        column = jnp.broadcast_to(row, (128, 128)).T[:NPIT, :]
+        return jnp.concatenate([
+            jnp.sum(jnp.where(ids == pit[i:i + 1, :], column, f32(0)), axis=0, keepdims=True)
+            for i in range(rows)
+        ], axis=0)
+
+    def by_pit(first_field, second_field):
+        one, two = jnp.zeros((NPIT, 128), f32), jnp.zeros((NPIT, 128), f32)
+        for i in range(rows):
+            hit = ids == pit[i:i + 1, :]
+            one = one + jnp.where(hit, first_field[i:i + 1, :], f32(0))
+            two = two + jnp.where(hit, second_field[i:i + 1, :], f32(0))
+        return jnp.sum(jnp.concatenate([one, two], axis=0).T, axis=0, keepdims=True)
 
     inpit = pit < NPIT
     lake_row = lake_ref[...]
@@ -229,8 +231,7 @@
     top_rows = pl.ds(0, rows)
     DG[top_rows, :] += jnp.where(inpit, f32(LEAK), f32(0))
     R[top_rows, :] += rain + jnp.where(inpit, LEAK * (lake_cell - top_h), f32(0))
-    r8 = lax.broadcasted_iota(jnp.int32, (8, rows * 128), 0)
-    early = by_pit(jnp.where(r8 == 0, flatten(rain), jnp.where(r8 == 1, f32(1), flatten(top_h))))
+    rain_area = by_pit(rain, jnp.ones((rows, 128), f32))
 
     receive("x", xs1, xr1, 0)
     tx_low = harmonic(c_first, xr1[0, 0])
@@ -277,8 +278,7 @@
         out = out + ty * ry(z, -1) + ry(ty * z, 1)
         put0(NZ, k, out + get(TZ, k) * get(Z, k, 1) + get(TZ, k, -1) * get(Z, k, -1))
 
-    ones8 = jnp.zeros((8, rows * 128), f32)
-    mid = by_pit(flatten(Z[pl.ds(lo_pad, rows), :]) + ones8)
+    z_head = by_pit(Z[pl.ds(lo_pad, rows), :], top_h)
 
     receive("x", xs2, xr2, 4)
     NZ[first, :] += tx_low * xr2[0]
@@ -306,7 +306,8 @@
         return acc + u * inner
 
     acc_f = lax.fori_loop(0, steps, make_f, zero_acc)
-    late = by_pit(flatten(U[pl.ds(lo_pad, rows), :]) + ones8)
+    top_u = U[pl.ds(lo_pad, rows), :]
+    u_sum = by_pit(top_u, jnp.zeros((rows, 128), f32))
 
     def row_sum(acc):
         return jnp.sum(jnp.sum(acc, axis=0), axis=0, keepdims=True)
@@ -325,7 +326,9 @@
     l1 = lax.broadcasted_iota(jnp.int32, (8, 128), 1)
     scal = jnp.where(r1 == 0, sum_a, jnp.where(r1 == 1, sum_g, jnp.where(r1 == 2, sum_c, sum_f)))
     scal = scal + pltpu.roll(scal, 64, 1)
-    pits = jnp.where(r1 < 3, early, jnp.where(r1 == 3, mid, late))
+    pits = jnp.where(r1 < 2, rain_area, jnp.where(r1 < 4, z_head, u_sum))
+    swapped = (r1 == 1) | (r1 == 2)
+    pits = jnp.where(swapped, pltpu.roll(pits, 128 - NPIT, 1), pits)
     gather[me] = jnp.where(l1 < NPIT, pits, scal)
 
     def reduce_copy(s):
@@ -418,7 +421,7 @@
                 pltpu.SMEM(ksat_table.shape, f32), pltpu.SMEM(ksat_table.shape, f32), pltpu.SMEM(ksat_table.shape, f32),
                 pltpu.VMEM((rows, width), f32), pltpu.VMEM((1, NPIT), f32), pltpu.VMEM((rows, width), jnp.int32),
                 padded, pltpu.VMEM((cells, width), jnp.int32), padded, block, block, block, padded,
-                block, padded, block, padded, pltpu.VMEM((128, rows * 128), f32),
+                block, padded, block, padded,
                 pltpu.VMEM((2, 2, lz, width), f32), pltpu.VMEM((2, 2, lz, width), f32),
                 pltpu.VMEM((2, 2, cells), f32), pltpu.VMEM((2, 2, cells), f32),
                 pltpu.VMEM((2, lz, width), f32), pltpu.VMEM((2, lz, width), f32),
@@ -440,7 +443,14 @@
                 ksat_table, alpha_table, capacity_table, rain, lake_level.reshape(1, NPIT), pit_id,
             ))
         )
-        out, boundary, lake_new = results
+        out, boundary, lake_new = pl.pallas_call(
+            write_out,
+            out_shape=shapes,
+            in_specs=[vmem] * 3,
+            out_specs=(hbm,) * 3,
+            scratch_shapes=[pltpu.SemaphoreType.DMA((3,))],
+            name="write",
+        )(*(pltpu.with_memory_space_constraint(x, pltpu.VMEM) for x in results))
         return out.reshape(lz, rows, width), boundary, lake_new.reshape(NPIT)
 
     return jax.shard_map(

time: 23 us -> 21 us (0.913)
  local copies, waits for them, and re-layouts: 1.84 us -> 0 us
    unnamed x3 -> x0, local copies, waits for them, and re-layouts: 1.84 us -> none
    pallas_call x1, Pallas kernels: 20.4 us -> 19.4 us  [shards(): pl.pallas_call(functools.partial(kernel, nx, ny, lz, rows), out_shape=sha...]
    pallas_call x0 -> x1, Pallas kernels: none -> 0.76 us  [shards(): pl.pallas_call(write_out, out_shape=shapes, in_specs=[vmem] * 3, out_spec...]
where the time goes in v3:
time: 21 us; the launch traced here: 20.8 us
  Pallas kernels  20.2 us (96%)
  between operations  0.64 us (3%)
    pallas_call x1, Pallas kernels, shards(): pl.pallas_call(functools.partial(kernel, nx, ny, lz, rows), out_shape=sha...  19.4 us
    pallas_call x1, Pallas kernels, shards(): pl.pallas_call(write_out, out_shape=shapes, in_specs=[vmem] * 3, out_spec...  0.76 us

profile of v3, /device:TPU:0, one launch (start us, length us, event | category | flops | bytes accessed | tf_op | source)
XLA Modules:
  0.0 20.8 jit_solution(5022888937255760110)
XLA Ops:
  0.6 19.4 %step.1 = (f32[640,128]{1,0:T(8,128)S(1)}, f32[16,128]{1,0:T(8,128)S(1)}, f32[1,64]{1,0:T(1,128)S(1)}) custom-call(f32[640,128]{1,0:T(8,128)} %bitcast.5, s32[640,128]{1,0:T(8,128)} %bitcast.6, f32[12]{0:T(128)} %ksat_hbm.1, f32[12]{0:T(128)} %alpha_hbm.1, f32[12]{0:T(128)} %cap_hbm.1, f32[16,128]{1,0:T(8,128)} %rain_hbm.1, f32[1,64]{1,0:T(1,128)} %bitcast.7, ...), custom_call_target="tpu_custom_call" | custom-call | tf_op jit(solution)/shard_map/step/pallas_call | solution.py:415
  20.1 0.8 %write.1 = (f32[640,128]{1,0:T(8,128)}, f32[16,128]{1,0:T(8,128)}, f32[1,64]{1,0:T(1,128)}) custom-call(f32[640,128]{1,0:T(8,128)S(1)} %get-tuple-element.9.a_ref, f32[16,128]{1,0:T(8,128)S(1)} %get-tuple-element.10.b_ref, f32[1,64]{1,0:T(1,128)S(1)} %get-tuple-element.11.c_ref), custom_call_target="tpu_custom_call" | custom-call | tf_op jit(solution)/shard_map/write/pallas_call | solution.py:446

commit v4 on v3

--- a/solution.py
+++ b/solution.py
@@ -10,7 +10,7 @@
 NPIT = 64
 LEAK = 0.5
 VERT = 2.0
-CH = 20
+CH = 40
 MESH = pl.DeviceIdType.MESH
 
 
@@ -121,9 +121,7 @@
     in_s.wait()
     in_h.wait()
 
-    @pl.loop(0, steps)
-    def _(k):
-        classes = SC[at0(k), :]
+    def soil(classes, head):
         ks = jnp.zeros(classes.shape, f32)
         al = jnp.zeros(classes.shape, f32)
         cp = jnp.zeros(classes.shape, f32)
@@ -132,17 +130,25 @@
             ks = jnp.where(match, ksat_ref[which], ks)
             al = jnp.where(match, alpha_ref[which], al)
             cp = jnp.where(match, cap_ref[which], cp)
-        relative = jnp.exp(al * jnp.minimum(H[at(k), :], 0.0))
-        C[at(k), :] = ks * relative
-        DG[at0(k), :] = cp * relative
+        relative = jnp.exp(al * jnp.minimum(head, 0.0))
+        return ks * relative, cp * relative
 
     def edge(ref, which, pad):
         return ref[pl.ds(pad + which, lz, stride=rows), :]
 
-    c_first, c_last = edge(C, 0, lo_pad), edge(C, rows - 1, lo_pad)
     h_first, h_last = edge(H, 0, lo_pad), edge(H, rows - 1, lo_pad)
+    c_first, _ = soil(edge(SC, 0, 0), h_first)
+    c_last, _ = soil(edge(SC, rows - 1, 0), h_last)
     xs1[0, 0], xs1[0, 1] = c_first, h_first
     xs1[1, 0], xs1[1, 1] = c_last, h_last
+    pl.semaphore_wait(barrier, n - 1)
+    send("x", xs1, xr1, 0)
+
+    @pl.loop(0, steps)
+    def _(k):
+        cond, store = soil(SC[at0(k), :], H[at(k), :])
+        C[at(k), :] = cond
+        DG[at0(k), :] = store
 
     def columns(ref, pad):
         turned = ref[pl.ds(pad, cells), :].T
@@ -154,8 +160,6 @@
         bottom = jnp.where(r == 7, high, f32(0))
         return jnp.concatenate([top, jnp.zeros((112, cells), f32), bottom], axis=0).T
 
-    pl.semaphore_wait(barrier, n - 1)
-    send("x", xs1, xr1, 0)
     cy = columns(C, lo_pad)
     hy = columns(H, lo_pad)
     for side in (0, 1):
@@ -250,6 +254,11 @@
         ty_low * (yr1[0, 1:2, :] - hy[0]), ty_high * (yr1[1, 1:2, :] - hy[1])
     )
 
+    for side, row in ((0, 0), (1, rows - 1)):
+        inverse_row = 1.0 / (edge(DG, row, 0) + edge(NZ, row, 0))
+        xs2[side] = (edge(R, row, 0) + edge(U, row, lo_pad)) * inverse_row
+    send("x", xs2, xr2, 4)
+
     zero_acc = jnp.zeros(shape3, f32)
 
     def make_z(k, acc):
@@ -263,9 +272,6 @@
 
     acc_a = lax.fori_loop(0, steps, make_z, zero_acc)
 
-    xs2[0] = edge(Z, 0, lo_pad)
-    xs2[1] = edge(Z, rows - 1, lo_pad)
-    send("x", xs2, xr2, 4)
     zy = columns(Z, lo_pad)
     for side in (0, 1):
         ys2[side] = zy[side]
@@ -286,6 +292,9 @@
     receive("y", ys2, yr2, 6)
     U[pl.ds(lo_pad, cells), :] = to_block(ty_low * yr2[0], ty_high * yr2[1])
 
+    xs3[0] = (edge(NZ, 0, 0) + edge(U, 0, lo_pad)) * edge(DG, 0, 0)
+    send("x", xs3, xr3, 8, (0,))
+
     def make_u(k, acc):
         nz = get0(NZ, k) + get(U, k)
         u = nz * get0(DG, k)
@@ -294,8 +303,6 @@
 
     acc_g, acc_c = lax.fori_loop(0, steps, make_u, (zero_acc, zero_acc))
 
-    xs3[0] = edge(U, 0, lo_pad)
-    send("x", xs3, xr3, 8, (0,))
     uy = columns(U, lo_pad)
     ys3[0] = uy[0]
     send("y", ys3, yr3, 10, (0,))

time: 21 us -> 20.5 us (0.976)
  Pallas kernels: 20.2 us -> 19.8 us
    pallas_call x1, Pallas kernels: 19.4 us -> 19 us  [shards(): pl.pallas_call(functools.partial(kernel, nx, ny, lz, rows), out_shape=sha...]
where the time goes in v4:
time: 20.5 us; the launch traced here: 20.4 us
  Pallas kernels  19.8 us (97%)
  between operations  0.64 us (3%)
    pallas_call x1, Pallas kernels, shards(): pl.pallas_call(functools.partial(kernel, nx, ny, lz, rows), out_shape=sha...  19 us
    pallas_call x1, Pallas kernels, shards(): pl.pallas_call(write_out, out_shape=shapes, in_specs=[vmem] * 3, out_spec...  0.76 us

profile of v4, /device:TPU:0, one launch (start us, length us, event | category | flops | bytes accessed | tf_op | source)
XLA Modules:
  0.0 20.4 jit_solution(5787305734281883375)
XLA Ops:
  0.6 19.0 %step.1 = (f32[640,128]{1,0:T(8,128)S(1)}, f32[16,128]{1,0:T(8,128)S(1)}, f32[1,64]{1,0:T(1,128)S(1)}) custom-call(f32[640,128]{1,0:T(8,128)} %bitcast.5, s32[640,128]{1,0:T(8,128)} %bitcast.6, f32[12]{0:T(128)} %ksat_hbm.1, f32[12]{0:T(128)} %alpha_hbm.1, f32[12]{0:T(128)} %cap_hbm.1, f32[16,128]{1,0:T(8,128)} %rain_hbm.1, f32[1,64]{1,0:T(1,128)} %bitcast.7, ...), custom_call_target="tpu_custom_call" | custom-call | tf_op jit(solution)/shard_map/step/pallas_call | solution.py:422
  19.6 0.8 %write.1 = (f32[640,128]{1,0:T(8,128)}, f32[16,128]{1,0:T(8,128)}, f32[1,64]{1,0:T(1,128)}) custom-call(f32[640,128]{1,0:T(8,128)S(1)} %get-tuple-element.9.a_ref, f32[16,128]{1,0:T(8,128)S(1)} %get-tuple-element.10.b_ref, f32[1,64]{1,0:T(1,128)S(1)} %get-tuple-element.11.c_ref), custom_call_target="tpu_custom_call" | custom-call | tf_op jit(solution)/shard_map/write/pallas_call | solution.py:453

commit v5 on v4

--- a/solution.py
+++ b/solution.py
@@ -235,7 +235,7 @@
     top_rows = pl.ds(0, rows)
     DG[top_rows, :] += jnp.where(inpit, f32(LEAK), f32(0))
     R[top_rows, :] += rain + jnp.where(inpit, LEAK * (lake_cell - top_h), f32(0))
-    rain_area = by_pit(rain, jnp.ones((rows, 128), f32))
+    supply_area = by_pit(rain + LEAK * top_h, jnp.ones((rows, 128), f32))
 
     receive("x", xs1, xr1, 0)
     tx_low = harmonic(c_first, xr1[0, 0])
@@ -284,7 +284,7 @@
         out = out + ty * ry(z, -1) + ry(ty * z, 1)
         put0(NZ, k, out + get(TZ, k) * get(Z, k, 1) + get(TZ, k, -1) * get(Z, k, -1))
 
-    z_head = by_pit(Z[pl.ds(lo_pad, rows), :], top_h)
+    z_sum = by_pit(Z[pl.ds(lo_pad, rows), :], jnp.zeros((rows, 128), f32))
 
     receive("x", xs2, xr2, 4)
     NZ[first, :] += tx_low * xr2[0]
@@ -329,14 +329,15 @@
         sum_f = sum_f + cross[:, i * 128:(i + 1) * 128]
     sum_f = 2.0 * sum_f
 
-    r1 = lax.broadcasted_iota(jnp.int32, (8, 128), 0)
-    l1 = lax.broadcasted_iota(jnp.int32, (8, 128), 1)
-    scal = jnp.where(r1 == 0, sum_a, jnp.where(r1 == 1, sum_g, jnp.where(r1 == 2, sum_c, sum_f)))
-    scal = scal + pltpu.roll(scal, 64, 1)
-    pits = jnp.where(r1 < 2, rain_area, jnp.where(r1 < 4, z_head, u_sum))
-    swapped = (r1 == 1) | (r1 == 2)
-    pits = jnp.where(swapped, pltpu.roll(pits, 128 - NPIT, 1), pits)
-    gather[me] = jnp.where(l1 < NPIT, pits, scal)
+    half = lax.broadcasted_iota(jnp.int32, (1, 128), 1) < NPIT
+
+    def fold(row):
+        return row + pltpu.roll(row, 64, 1)
+
+    gather[me, 0:1, :] = supply_area
+    gather[me, 1:2, :] = jnp.where(half, z_sum, fold(sum_a))
+    gather[me, 2:3, :] = jnp.where(half, u_sum, fold(sum_g))
+    gather[me, 3:4, :] = jnp.where(half, fold(sum_c), fold(sum_f))
 
     def reduce_copy(s):
         return pltpu.make_async_remote_copy(
@@ -360,8 +361,11 @@
     else:
         total = lax.fori_loop(1, n, lambda j, t: t + gather[j], gather[0])
 
-    scalars = jnp.sum(jnp.where(l1 < NPIT, f32(0), total), axis=1, keepdims=True)
-    a, g, c, f = (scalars[i:i + 1, :] for i in range(4))
+    def half_sum(row, low):
+        return jnp.sum(jnp.where(half == low, row, f32(0)), axis=1, keepdims=True)
+
+    a, g = half_sum(total[1:2, :], False), half_sum(total[2:3, :], False)
+    c, f = half_sum(total[3:4, :], True), half_sum(total[3:4, :], False)
     b = a - g
     step0 = a / b
     ratio = (a * c - g * g) / (b * b)
@@ -376,10 +380,10 @@
     def _(k):
         put0(out_ref, k, get(H, k) + coef_z3 * get(Z, k) + coef_u3 * get(U, k))
 
-    inflow, area = total[0:1, :NPIT], total[1:2, :NPIT]
-    top_sum = total[2:3, :NPIT] + coef_z * total[3:4, :NPIT] + coef_u * total[4:5, :NPIT]
-    outflow = LEAK * (lake_row * area - top_sum)
-    lake_new = lake_row + (inflow - outflow) / jnp.maximum(area, 1.0)
+    supply = total[0:1, :NPIT]
+    area = pltpu.roll(total, 64, 1)[0:1, :NPIT]
+    change = coef_z * total[1:2, :NPIT] + coef_u * total[2:3, :NPIT]
+    lake_new = lake_row + (supply + LEAK * (change - lake_row * area)) / jnp.maximum(area, 1.0)
     lake_out_ref[...] = lake_new
     lake_new_cell = spread(jnp.concatenate([lake_new, jnp.zeros((1, 128 - NPIT), f32)], axis=1))
     bnd_ref[...] = jnp.where(inpit, lake_new_cell, out_ref[pl.ds(0, rows), :])
@@ -435,7 +439,7 @@
                 pltpu.VMEM((2, 1, cells), f32), pltpu.VMEM((2, 1, cells), f32),
                 pltpu.VMEM((2, lz, width), f32), pltpu.VMEM((2, lz, width), f32),
                 pltpu.VMEM((2, 1, cells), f32), pltpu.VMEM((2, 1, cells), f32),
-                pltpu.VMEM((n, 8, 128), f32),
+                pltpu.VMEM((n, 4, 128), f32),
                 pltpu.SemaphoreType.DMA((8,)),
                 pltpu.SemaphoreType.DMA((12,)), pltpu.SemaphoreType.DMA((12,)),
                 pltpu.SemaphoreType.DMA((n,)), pltpu.SemaphoreType.DMA((n,)),

time: 20.5 us -> 20.5 us (level)
  no operation moved by 1% of the time
where the time goes in v5:
time: 20.5 us; the launch traced here: 20.3 us
  Pallas kernels  19.7 us (96%)
  between operations  0.64 us (3%)
    pallas_call x1, Pallas kernels, shards(): pl.pallas_call(functools.partial(kernel, nx, ny, lz, rows), out_shape=sha...  18.9 us
    pallas_call x1, Pallas kernels, shards(): pl.pallas_call(write_out, out_shape=shapes, in_specs=[vmem] * 3, out_spec...  0.76 us

profile of v5, /device:TPU:0, one launch (start us, length us, event | category | flops | bytes accessed | tf_op | source)
XLA Modules:
  0.0 20.3 jit_solution(10743631131865575986)
XLA Ops:
  0.6 18.9 %step.1 = (f32[640,128]{1,0:T(8,128)S(1)}, f32[16,128]{1,0:T(8,128)S(1)}, f32[1,64]{1,0:T(1,128)S(1)}) custom-call(f32[640,128]{1,0:T(8,128)} %bitcast.5, s32[640,128]{1,0:T(8,128)} %bitcast.6, f32[12]{0:T(128)} %ksat_hbm.1, f32[12]{0:T(128)} %alpha_hbm.1, f32[12]{0:T(128)} %cap_hbm.1, f32[16,128]{1,0:T(8,128)} %rain_hbm.1, f32[1,64]{1,0:T(1,128)} %bitcast.7, ...), custom_call_target="tpu_custom_call" | custom-call | tf_op jit(solution)/shard_map/step/pallas_call | solution.py:426
  19.5 0.8 %write.1 = (f32[640,128]{1,0:T(8,128)}, f32[16,128]{1,0:T(8,128)}, f32[1,64]{1,0:T(1,128)}) custom-call(f32[640,128]{1,0:T(8,128)S(1)} %get-tuple-element.9.a_ref, f32[16,128]{1,0:T(8,128)S(1)} %get-tuple-element.10.b_ref, f32[1,64]{1,0:T(1,128)S(1)} %get-tuple-element.11.c_ref), custom_call_target="tpu_custom_call" | custom-call | tf_op jit(solution)/shard_map/write/pallas_call | solution.py:457
